TPU v7x, 32 devices: a whole 2x2x4 slice. The times are simulated.
32 devices in a mesh: seq: 8 (over z, y), head: 4 (over x, core).
Axes of the slice: x: 2, y: 2, z: 4, core: 2. Of those that a mesh axis runs over, the one named last changes fastest.
Arguments:
- tokens: bfloat16 [16384, 512], P('seq'), may hold values from -6 to 6
- cotangent: bfloat16 [16384, 512], P('seq'), may hold values from -6 to 6
- frames: int32 [32], replicated, may hold values from 1 to 16, 256 in all
- qkv_weight: float32 [3, 512, 512], P(None, 'seq', 'head'), may hold values from -0.53033009 to 0.53033009
- qkv_first: float32 [3, 512, 512], P(None, 'seq', 'head'), may hold values from -224 to 224
- qkv_second: float32 [3, 512, 512], P(None, 'seq', 'head'), may hold values from 491.52 to 9830.4
- out_weight: float32 [512, 512], P('head', 'seq'), may hold values from -3 to 3
- out_first: float32 [512, 512], P('head', 'seq'), may hold values from -56 to 56
- out_second: float32 [512, 512], P('head', 'seq'), may hold values from 26.2144 to 524.288
- up_weight: float32 [512, 2048], P('seq', 'head'), may hold values from -0.53033009 to 0.53033009
- up_first: float32 [512, 2048], P('seq', 'head'), may hold values from -192 to 192
- up_second: float32 [512, 2048], P('seq', 'head'), may hold values from 327.68 to 6717.44
- down_weight: float32 [2048, 512], P('head', 'seq'), may hold values from -0.26516504 to 0.26516504
- down_first: float32 [2048, 512], P('head', 'seq'), may hold values from -320 to 320
- down_second: float32 [2048, 512], P('head', 'seq'), may hold values from 851.968 to 17203.2
- norm_params: float32 [4, 512], P(None, 'seq'), may hold values from -1 to 1.8, as said below
- norm_first: float32 [4, 512], P(None, 'seq'), may hold values from -768 to 768
- norm_second: float32 [4, 512], P(None, 'seq'), may hold values from 5406.72 to 108134.4
Outputs:
- block_out: bfloat16 [16384, 512], P('seq')
- input_grad: float32 [16384, 512], P('seq')
- qkv_grad: float32 [3, 512, 512], P(None, 'seq', 'head')
- qkv_first_new: float32 [3, 512, 512], P(None, 'seq', 'head')
- qkv_second_new: float32 [3, 512, 512], P(None, 'seq', 'head')
- qkv_new: float32 [3, 512, 512], P(None, 'seq', 'head')
- qkv_copy: bfloat16 [3, 512, 512], P(None, 'seq', 'head')
- out_grad: float32 [512, 512], P('head', 'seq')
- out_first_new: float32 [512, 512], P('head', 'seq')
- out_second_new: float32 [512, 512], P('head', 'seq')
- out_new: float32 [512, 512], P('head', 'seq')
- out_copy: bfloat16 [512, 512], P('head', 'seq')
- up_grad: float32 [512, 2048], P('seq', 'head')
- up_first_new: float32 [512, 2048], P('seq', 'head')
- up_second_new: float32 [512, 2048], P('seq', 'head')
- up_new: float32 [512, 2048], P('seq', 'head')
- up_copy: bfloat16 [512, 2048], P('seq', 'head')
- down_grad: float32 [2048, 512], P('head', 'seq')
- down_first_new: float32 [2048, 512], P('head', 'seq')
- down_second_new: float32 [2048, 512], P('head', 'seq')
- down_new: float32 [2048, 512], P('head', 'seq')
- down_copy: bfloat16 [2048, 512], P('head', 'seq')
- norm_grad: float32 [4, 512], P(None, 'seq')
- norm_first_new: float32 [4, 512], P(None, 'seq')
- norm_second_new: float32 [4, 512], P(None, 'seq')
- norm_new: float32 [4, 512], P(None, 'seq')
- norm_copy: bfloat16 [4, 512], P(None, 'seq')
- norms: float32 [5, 2], replicated
Inputs may be any that keep to these rules, and one draw needn't show every extreme that they name: frames of each clip, summing to 256; the longest clip has exactly 16. `norm_params`: gains positive, shifts of either sign.
All inputs are finite; a program needn't handle non-finite values.
Results may differ from a plain program's by a relative error of at most 0.012.
The roundings to bfloat16 on the way count: a program that leaves them out, or rounds other values in their place, can miss the bound.
Values may be sent and summed in bfloat16 or wider, within the bound.
A program may use at most 320 MiB of HBM per device.

v0:
```python
import jax
import jax.numpy as jnp
from jax import lax
from jax.sharding import PartitionSpec as P

HEAD_DIM = 64
FRAME_TOKENS = 64
MOST_FRAMES = 16
STEP = 5


EPS_NORM = 1e-05
BETA_ONE = 0.5
BETA_TWO = 0.6
RATE = 0.3
DECAY = 0.01
EPS_ADAM = 1e-06
MASKED = -1e30


def passed_along(block, axis, distance):
    devices = range(lax.axis_size(axis))
    route = [(i - distance, i) for i in devices if i - distance in devices]
    return lax.ppermute(block, axis, route)


def normalize(values, gain_row, shift_row):
    average = jnp.mean(values, axis=-1, keepdims=True)
    centered = values - average
    variance = jnp.mean(centered * centered, axis=-1, keepdims=True)
    inverse = lax.rsqrt(variance + EPS_NORM)
    normed = centered * inverse
    return (normed * gain_row + shift_row, normed, inverse)


def norm_back(gradient, normed, inverse, gain_row):
    scaled = gradient * gain_row
    return inverse * (
        scaled
        - jnp.mean(scaled, axis=-1, keepdims=True)
        - normed * jnp.mean(scaled * normed, axis=-1, keepdims=True)
    )


def clip_of(positions, clip_ends):
    frame_index = positions // FRAME_TOKENS
    return jnp.sum((frame_index[:, None] >= clip_ends[None, :]).astype(jnp.int32), axis=1)


def allowed_pairs(query_pos, key_pos, clip_ends, total_rows):
    query_inside = (query_pos >= 0) & (query_pos < total_rows)
    key_inside = (key_pos >= 0) & (key_pos < total_rows)
    same_clip = clip_of(query_pos, clip_ends)[:, None] == clip_of(key_pos, clip_ends)[None, :]
    earlier = (key_pos // FRAME_TOKENS)[None, :] <= (query_pos // FRAME_TOKENS)[:, None]
    return query_inside[:, None] & key_inside[None, :] & same_clip & earlier


def scores_for(queries, keys, allowed, score_scale):
    raw_scores = (
        jnp.einsum("qhd,khd->hqk", queries, keys, preferred_element_type=jnp.float32) * score_scale
    )
    return jnp.where(allowed[None], raw_scores, MASKED)


def squares_of(arrays, head_first):
    summed = jnp.stack([jnp.sum(member * member) for member in arrays])
    weighting = jnp.stack(
        [jnp.float32(1.0), jnp.float32(1.0), jnp.float32(1.0), jnp.float32(1.0), head_first]
    )
    return summed * weighting


def local(
    tokens,
    cotangent,
    frames,
    qkv_weight,
    qkv_first,
    qkv_second,
    out_weight,
    out_first,
    out_second,
    up_weight,
    up_first,
    up_second,
    down_weight,
    down_first,
    down_second,
    norm_params,
    norm_first,
    norm_second,
):
    rows_dev = tokens.shape[0]
    seq_count = lax.axis_size("seq")
    total_rows = rows_dev * seq_count
    frames_dev = rows_dev // FRAME_TOKENS
    reach_back = min((MOST_FRAMES + frames_dev - 2) // frames_dev, seq_count - 1)
    window_rows = (reach_back + 1) * rows_dev
    heads_local = qkv_weight.shape[2] // HEAD_DIM
    score_scale = HEAD_DIM ** (-0.5)
    clip_ends = jnp.cumsum(frames)
    seq_index = lax.axis_index("seq")
    query_pos = seq_index * rows_dev + jnp.arange(rows_dev, dtype=jnp.int32)
    window_pos = (seq_index - reach_back) * rows_dev + jnp.arange(window_rows, dtype=jnp.int32)
    head_first = jnp.where(lax.axis_index("head") == 0, 1.0, 0.0).astype(jnp.float32)
    masters = (qkv_weight, out_weight, up_weight, down_weight, norm_params)
    copies = tuple((master.astype(jnp.bfloat16) for master in masters))
    full_qkv, full_out, full_up, full_down, full_norm = (
        lax.all_gather(copies[0], "seq", axis=1, tiled=True),
        lax.all_gather(copies[1], "seq", axis=1, tiled=True),
        lax.all_gather(copies[2], "seq", axis=0, tiled=True),
        lax.all_gather(copies[3], "seq", axis=1, tiled=True),
        lax.all_gather(copies[4], "seq", axis=1, tiled=True),
    )
    gains = full_norm.astype(jnp.float32)
    inputs = tokens.astype(jnp.float32)
    first, first_normed, first_inv = normalize(inputs, gains[0], gains[1])
    first_low = first.astype(jnp.bfloat16)
    projected = jnp.einsum(
        "td,sde->ste", first_low, full_qkv, preferred_element_type=jnp.float32
    ).astype(jnp.bfloat16)
    queries = projected[0]
    keys_local = projected[1]
    values_local = projected[2]
    local_pair = jnp.stack([keys_local, values_local])
    distance = 1
    earlier_pairs = [passed_along(local_pair, "seq", distance)]
    window_pair = jnp.concatenate(earlier_pairs[::-1] + [local_pair], axis=1)
    query_heads = queries.reshape(rows_dev, heads_local, HEAD_DIM)
    key_heads = window_pair[0].reshape(window_rows, heads_local, HEAD_DIM)
    value_heads = window_pair[1].reshape(window_rows, heads_local, HEAD_DIM)
    allowed = allowed_pairs(query_pos, window_pos, clip_ends, total_rows)
    scores = scores_for(query_heads, key_heads, allowed, score_scale)
    highest = jnp.max(scores, axis=-1)
    log_total = highest + jnp.log(jnp.sum(jnp.exp(scores - highest[..., None]), axis=-1))
    probability_low = jnp.exp(scores - log_total[..., None]).astype(jnp.bfloat16)
    attended = jnp.einsum(
        "hqk,khd->qhd", probability_low, value_heads, preferred_element_type=jnp.float32
    )
    attended_low = attended.reshape(rows_dev, heads_local * HEAD_DIM).astype(jnp.bfloat16)
    attn_out = lax.psum(jnp.dot(attended_low, full_out, preferred_element_type=jnp.float32), "head")
    resid = inputs + attn_out
    second, second_normed, second_inv = normalize(resid, gains[2], gains[3])
    second_low = second.astype(jnp.bfloat16)
    upper = jnp.dot(second_low, full_up, preferred_element_type=jnp.float32)
    active_low = jax.nn.gelu(upper, approximate=True).astype(jnp.bfloat16)
    mlp_out = lax.psum(jnp.dot(active_low, full_down, preferred_element_type=jnp.float32), "head")
    output = (resid + mlp_out).astype(jnp.bfloat16)
    grad_down = jnp.dot(active_low.T, cotangent, preferred_element_type=jnp.float32)
    grad_active = jnp.dot(cotangent, full_down.T, preferred_element_type=jnp.float32)
    gelu_value, gelu_pull = jax.vjp(lambda inner: jax.nn.gelu(inner, approximate=True), upper)
    grad_upper = gelu_pull(grad_active)[0].astype(jnp.bfloat16)
    grad_up = jnp.dot(second_low.T, grad_upper, preferred_element_type=jnp.float32)
    grad_second = lax.psum(
        jnp.dot(grad_upper, full_up.T, preferred_element_type=jnp.float32), "head"
    )
    grad_resid = cotangent.astype(jnp.float32) + norm_back(
        grad_second, second_normed, second_inv, gains[2]
    )
    gain_two = jnp.sum(grad_second * second_normed, axis=0)
    shift_two = jnp.sum(grad_second, axis=0)
    grad_attn = grad_resid.astype(jnp.bfloat16)
    grad_out_w = jnp.dot(attended_low.T, grad_attn, preferred_element_type=jnp.float32)
    grad_attended = jnp.dot(grad_attn, full_out.T, preferred_element_type=jnp.float32).astype(
        jnp.bfloat16
    )
    grad_att_heads = grad_attended.reshape(rows_dev, heads_local, HEAD_DIM)
    again = scores_for(query_heads, key_heads, allowed, score_scale)
    probability = jnp.exp(again - log_total[..., None])
    grad_prob = jnp.einsum(
        "qhd,khd->hqk", grad_att_heads, value_heads, preferred_element_type=jnp.float32
    )
    delta = jnp.sum(probability * grad_prob, axis=-1)
    grad_scores = (probability * (grad_prob - delta[..., None])).astype(jnp.bfloat16)
    grad_query = (
        jnp.einsum("hqk,khd->qhd", grad_scores, key_heads, preferred_element_type=jnp.float32)
        * score_scale
    )
    grad_key = (
        jnp.einsum("hqk,qhd->khd", grad_scores, query_heads, preferred_element_type=jnp.float32)
        * score_scale
    )
    grad_value = jnp.einsum(
        "hqk,qhd->khd",
        probability.astype(jnp.bfloat16),
        grad_att_heads,
        preferred_element_type=jnp.float32,
    )
    window_terms = jnp.stack(
        [grad_key.reshape(window_rows, -1), grad_value.reshape(window_rows, -1)]
    )
    key_terms = window_terms[:, reach_back * rows_dev :]
    distance = 1
    start_row = (reach_back - distance) * rows_dev
    piece = window_terms[:, start_row : start_row + rows_dev]
    key_terms = key_terms + passed_along(piece, "seq", -distance)
    grad_stack = jnp.stack(
        [
            grad_query.reshape(rows_dev, -1).astype(jnp.bfloat16),
            key_terms[0].astype(jnp.bfloat16),
            key_terms[1].astype(jnp.bfloat16),
        ]
    )
    grad_qkv_w = jnp.einsum(
        "td,ste->sde", first_low, grad_stack, preferred_element_type=jnp.float32
    )
    grad_first = lax.psum(
        jnp.einsum("ste,sde->td", grad_stack, full_qkv, preferred_element_type=jnp.float32), "head"
    )
    input_grad = grad_resid + norm_back(grad_first, first_normed, first_inv, gains[0])
    gain_one = jnp.sum(grad_first * first_normed, axis=0)
    shift_one = jnp.sum(grad_first, axis=0)
    grad_norm_local = jnp.stack([gain_one, shift_one, gain_two, shift_two])
    grads = (
        lax.psum_scatter(grad_qkv_w, "seq", scatter_dimension=1, tiled=True),
        lax.psum_scatter(grad_out_w, "seq", scatter_dimension=1, tiled=True),
        lax.psum_scatter(grad_up, "seq", scatter_dimension=0, tiled=True),
        lax.psum_scatter(grad_down, "seq", scatter_dimension=1, tiled=True),
        lax.psum_scatter(grad_norm_local, "seq", scatter_dimension=1, tiled=True),
    )
    moments = (qkv_first, out_first, up_first, down_first, norm_first)
    squares = (qkv_second, out_second, up_second, down_second, norm_second)
    new_firsts = []
    new_seconds = []
    directions = []
    for master, moment, square, gradient in zip(masters, moments, squares, grads):
        new_first = BETA_ONE * moment + (1.0 - BETA_ONE) * gradient
        new_second = BETA_TWO * square + (1.0 - BETA_TWO) * gradient * gradient
        direction = (
            new_first
            / (1.0 - BETA_ONE**STEP)
            / (jnp.sqrt(new_second / (1.0 - BETA_TWO**STEP)) + EPS_ADAM)
            + DECAY * master
        )
        new_firsts.append(new_first)
        new_seconds.append(new_second)
        directions.append(direction)
    weight_squares, update_squares = lax.psum(
        (squares_of(masters, head_first), squares_of(directions, head_first)), ("seq", "head")
    )
    weight_norm = jnp.sqrt(weight_squares)
    update_norm = jnp.sqrt(update_squares)
    ratio = weight_norm / update_norm
    new_masters = [
        master - RATE * ratio[number] * direction
        for number, (master, direction) in enumerate(zip(masters, directions))
    ]
    norms = jnp.stack([weight_norm, update_norm], axis=1)
    return (
        output,
        input_grad,
        grads[0],
        new_firsts[0],
        new_seconds[0],
        new_masters[0],
        new_masters[0].astype(jnp.bfloat16),
        grads[1],
        new_firsts[1],
        new_seconds[1],
        new_masters[1],
        new_masters[1].astype(jnp.bfloat16),
        grads[2],
        new_firsts[2],
        new_seconds[2],
        new_masters[2],
        new_masters[2].astype(jnp.bfloat16),
        grads[3],
        new_firsts[3],
        new_seconds[3],
        new_masters[3],
        new_masters[3].astype(jnp.bfloat16),
        grads[4],
        new_firsts[4],
        new_seconds[4],
        new_masters[4],
        new_masters[4].astype(jnp.bfloat16),
        norms,
    )


def solution(mesh):
    in_specs = (
        P("seq", None),
        P("seq", None),
        P(),
        P(None, "seq", "head"),
        P(None, "seq", "head"),
        P(None, "seq", "head"),
        P("head", "seq"),
        P("head", "seq"),
        P("head", "seq"),
        P("seq", "head"),
        P("seq", "head"),
        P("seq", "head"),
        P("head", "seq"),
        P("head", "seq"),
        P("head", "seq"),
        P(None, "seq"),
        P(None, "seq"),
        P(None, "seq"),
    )
    out_specs = (
        P("seq", None),
        P("seq", None),
        P(None, "seq", "head"),
        P(None, "seq", "head"),
        P(None, "seq", "head"),
        P(None, "seq", "head"),
        P(None, "seq", "head"),
        P("head", "seq"),
        P("head", "seq"),
        P("head", "seq"),
        P("head", "seq"),
        P("head", "seq"),
        P("seq", "head"),
        P("seq", "head"),
        P("seq", "head"),
        P("seq", "head"),
        P("seq", "head"),
        P("head", "seq"),
        P("head", "seq"),
        P("head", "seq"),
        P("head", "seq"),
        P("head", "seq"),
        P(None, "seq"),
        P(None, "seq"),
        P(None, "seq"),
        P(None, "seq"),
        P(None, "seq"),
        P(),
    )
    return jax.shard_map(local, mesh=mesh, in_specs=in_specs, out_specs=out_specs, check_vma=False)
```

profile of v0, /device:TPU:0, one launch (start us, length us, event | category | flops | bytes accessed | tf_op | source)
XLA Modules:
  0.0 1129.2 jit_solution(6443802521503838267)
XLA Ops:
  8.1 22.3 %all-gather = bf16[8,64,4]{1,2,0:T(4,128)(2,1)S(1)} all-gather(bf16[1,64,4]{1,2,0:T(4,128)(2,1)S(1)} %convert_bitcast_fusion), channel_id=1, replica_groups=mesh['seq'=8,'head'=4] {'seq'}, dimensions={0}, use_global_device_ids=true | all-gather | bytes 4608 | tf_op jit(solution)/shard_map/all_gather | solution.py:113
  30.5 1.9 convert_reduce_fusion
  32.4 2.5 fusion.15
  35.6 31.1 %all_gather.16 = bf16[3,512,128]{2,1,0:T(8,128)(2,1)S(1)} all-gather(bf16[3,64,128]{2,1,0:T(8,128)(2,1)S(1)} %get-tuple-element.216), channel_id=1, replica_groups=mesh['seq'=8,'head'=4] {'seq'}, dimensions={1}, use_global_device_ids=true | all-gather | bytes 442368 | tf_op jit(solution)/shard_map/all_gather | solution.py:109
  66.7 1.9 fusion.23
  68.7 1.1 copy-done.19
  69.9 2.3 collective-permute-start
  72.8 13.0 %compare_and_fusion = pred[2048,4096]{1,0:T(8,128)(4,1)} fusion(s32[4096]{0:T(1024)S(1)} %add_select_fusion, s32[4096]{0:T(1024)S(1)} %convert_reduce_fusion.1, s32[2048]{0:T(1024)S(1)} %add_select_fusion.1, s32[2048]{0:T(1024)S(1)} %convert_reduce_fusion.2, pred[4096]{0:T(1024)(128)(4,1)S(1)} %fusion.44, pred[2048]{0:T(1024)(128)(4,1)S(1)} %fusion.50), kind=kLoop, calls=%fused_computation.7 | loop fusion | flops 41943040 | bytes 8443904 | tf_op jit(solution)/shard_map/and | solution.py:55
  85.8 1.1 slice.76
  87.0 37.6 %all_gather.17 = bf16[128,512]{0,1:T(8,128)(2,1)S(1)} all-gather(bf16[128,64]{0,1:T(8,128)(2,1)S(1)} %convert_element_type.121), channel_id=1, replica_groups=mesh['seq'=8,'head'=4] {'seq'}, dimensions={1}, use_global_device_ids=true | all-gather | bytes 147456 | tf_op jit(solution)/shard_map/all_gather | solution.py:110
  124.6 1.7 pad_maximum_fusion.2
  126.3 28.7 %fusion = (f32[2,2048]{1,0:T(2,128)S(1)}, f32[2,2048,4096]{2,1,0:T(8,128)}) fusion(pred[2048,4096]{1,0:T(8,128)(4,1)} %compare_and_fusion, bf16[2048,2,64]{0,2,1:T(8,128)(2,1)S(1)} %bitcast.95, bf16[4096,2,64]{0,2,1:T(8,128)(2,1)S(1)} %bitcast.93), kind=kOutput, calls=%fused_computation.5 | convolution fusion | flops 2197811200 | bytes 77086720 | tf_op jit(solution)/shard_map/qhd,khd->hqk/dot_general | solution.py:60
  155.1 24.1 %exponential_reduce_fusion = f32[2,2048]{1,0:T(2,128)S(1)} fusion(f32[2,2048,4096]{2,1,0:T(8,128)} %get-tuple-element.234, f32[2,2048]{1,0:T(2,128)S(1)} %get-tuple-element.233, pred[2048,4096]{1,0:T(8,128)(4,1)} %compare_and_fusion), kind=kLoop, calls=%fused_computation.3 | loop fusion | flops 67104768 | bytes 75530240 | tf_op jit(solution)/shard_map/reduce_sum | solution.py:135
  179.2 27.9 %convolution_convert_fusion.2 = bf16[2,64,2048]{2,1,0:T(8,128)(2,1)S(1)} fusion(bf16[4096,2,64]{0,2,1:T(8,128)(2,1)S(1)} %bitcast.98, f32[2,2048,4096]{2,1,0:T(8,128)} %get-tuple-element.234, f32[2,2048]{1,0:T(2,128)S(1)} %log_add_fusion, pred[2048,4096]{1,0:T(8,128)(4,1)} %compare_and_fusion), kind=kOutput, calls=%fused_computation.51 | convolution fusion | flops 2214854656 | bytes 77086720 | tf_op jit(solution)/shard_map/hqk,khd->qhd/dot_general | solution.py:137
  207.9 2.8 fusion.72
  210.7 31.4 %all_gather.18 = bf16[512,512]{1,0:T(8,128)(2,1)S(1)} all-gather(bf16[64,512]{1,0:T(8,128)(2,1)S(1)} %convert_element_type.123), channel_id=1, replica_groups=mesh['seq'=8,'head'=4] {'seq'}, dimensions={0}, use_global_device_ids=true | all-gather | bytes 589824 | tf_op jit(solution)/shard_map/all_gather | solution.py:111
  242.1 53.7 %all-reduce.9.cloned.1.call-done = f32[2048,512]{1,0:T(8,128)} async-done(((f32[2048,512]{1,0:T(8,128)}), f32[2048,512]{1,0:T(8,128)}) %all-reduce.9.cloned.1.call-update) | async-done | bytes 4194320 | tf_op jit(solution)/shard_map/psum | solution.py:141
  295.9 2.7 fusion.69
  300.5 1.3 fusion.73
  301.7 2.0 copy-done.9
  303.8 2.9 fusion.54
  306.7 63.7 %reduce-scatter.11.cloned.1.call-done = f32[512,64]{0,1:T(8,128)} async-done(((f32[512,512]{0,1:T(8,128)}), f32[512,64]{0,1:T(8,128)}) %reduce-scatter.11.cloned.1.call-update) | async-done | bytes 131088 | tf_op jit(solution)/shard_map/reduce_scatter | solution.py:218
  370.4 2.3 multiply_reduce_fusion.6
  372.7 31.5 %all_gather.19 = bf16[512,512]{0,1:T(8,128)(2,1)S(1)} all-gather(bf16[512,64]{0,1:T(8,128)(2,1)S(1)} %get-tuple-element.214), channel_id=1, replica_groups=mesh['seq'=8,'head'=4] {'seq'}, dimensions={1}, use_global_device_ids=true | all-gather | bytes 589824 | tf_op jit(solution)/shard_map/all_gather | solution.py:112
  404.3 5.6 fusion.22
  409.9 1.3 copy-done.12
  411.2 3.3 fusion.74
  414.6 3.8 fusion.75
  419.0 80.0 %all-reduce.11.cloned.1.call-done = f32[2048,512]{1,0:T(8,128)} async-done(((f32[2048,512]{1,0:T(8,128)}), f32[2048,512]{1,0:T(8,128)}) %all-reduce.11.cloned.1.call-update) | async-done | bytes 4194320 | tf_op jit(solution)/shard_map/psum | solution.py:154
  499.0 5.5 multiply_reduce_fusion.1
  504.9 3.5 multiply_add_fusion
  508.4 1.9 copy-done.2
  511.2 29.7 %fusion.56 = f32[2,64,4096]{2,1,0:T(8,128)} fusion(bf16[2048,2,64]{0,2,1:T(8,128)(2,1)S(1)} %bitcast.100, f32[2,2048,4096]{2,1,0:T(8,128)} %get-tuple-element.234, f32[2,2048]{1,0:T(2,128)S(1)} %log_add_fusion, pred[2048,4096]{1,0:T(8,128)(4,1)} %compare_and_fusion), kind=kOutput, calls=%fused_computation.152 | convolution fusion | flops 2214592512 | bytes 78135296 | tf_op jit(solution)/shard_map/hqk,qhd->khd/dot_general | solution.py:183
  540.9 50.7 %multiply_reduce_fusion = (f32[2,2048]{1,0:T(2,128)S(1)}, f32[2,2048,4096]{2,1,0:T(8,128)}) fusion(f32[2,2048,4096]{2,1,0:T(8,128)} %get-tuple-element.234, f32[2,2048]{1,0:T(2,128)S(1)} %log_add_fusion, pred[2048,4096]{1,0:T(8,128)(4,1)} %compare_and_fusion, bf16[2048,2,64]{0,2,1:T(8,128)(2,1)S(1)} %bitcast.101, bf16[4096,2,64]{0,2,1:T(8,128)(2,1)S(1)} %bitcast.99), kind=kOutput, calls=%fused_computation.1 | convolution fusion | flops 2231365632 | bytes 144211968 | tf_op jit(solution)/shard_map/qhd,khd->hqk/dot_general | solution.py:170
  591.6 1.9 copy.110
  593.6 56.0 %multiply_convert_fusion = bf16[2,2048,4096]{2,1,0:T(8,128)(2,1)} fusion(f32[2,2048,4096]{2,1,0:T(8,128)} %get-tuple-element.236, f32[2,2048,4096]{2,1,0:T(8,128)} %get-tuple-element.234, f32[2,2048]{1,0:T(2,128)S(1)} %get-tuple-element.235, f32[2,2048]{1,0:T(2,128)S(1)} %log_add_fusion, pred[2048,4096]{1,0:T(8,128)(4,1)} %compare_and_fusion), kind=kLoop, calls=%fused_computation | loop fusion | flops 100663296 | bytes 176193536 | tf_op jit(solution)/shard_map/convert_element_type | solution.py:174
  649.6 15.2 %convolution_multiply_fusion = f32[2,64,4096]{2,1,0:T(8,128)} fusion(bf16[2048,2,64]{0,2,1:T(8,128)(2,1)S(1)} %bitcast.96, bf16[2,2048,4096]{2,1,0:T(8,128)(2,1)} %multiply_convert_fusion), kind=kOutput, calls=%fused_computation.19 | convolution fusion | flops 2148007936 | bytes 36175872 | tf_op jit(solution)/shard_map/hqk,qhd->khd/dot_general | solution.py:180
  664.7 2.9 copy.109
  667.7 2.8 pad_maximum_fusion
  670.4 1.4 collective-permute-start.1
  671.9 15.5 %fusion.24 = bf16[2,64,2048]{2,1,0:T(8,128)(2,1)S(1)} fusion(bf16[4096,2,64]{0,2,1:T(8,128)(2,1)S(1)} %bitcast.94, bf16[2,2048,4096]{2,1,0:T(8,128)(2,1)} %multiply_convert_fusion), kind=kOutput, calls=%fused_computation.53 | convolution fusion | flops 2148007936 | bytes 35127296 | tf_op jit(solution)/shard_map/hqk,khd->qhd/dot_general | solution.py:176
  687.4 1.0 copy.111
  688.4 3.8 fusion.30
  692.3 28.4 %collective-permute-done.1 = f32[2,2048,128]{2,1,0:T(8,128)} collective-permute-done((f32[2,2048,128]{2,1,0:T(8,128)}, f32[2,2048,128]{2,1,0:T(8,128)}, u32[]{:S(2)}, u32[]{:S(2)}) %collective-permute-start.1) | collective-permute-done | bytes 2097184 | tf_op jit(solution)/shard_map/ppermute | solution.py:24
  720.7 2.4 fusion.27
  723.2 3.4 convolution_bitcast_fusion.1
  726.6 2.4 copy.113
  729.2 5.9 fusion.55
  735.1 3.3 convolution_bitcast_fusion
  740.4 2.3 multiply_reduce_fusion.7
  742.7 13.7 %reduce-scatter.7.cloned.1.call-done = f32[128,64]{0,1:T(8,128)} async-done(((f32[128,512]{0,1:T(8,128)}), f32[128,64]{0,1:T(8,128)}) %reduce-scatter.7.cloned.1.call-update) | async-done | bytes 32784 | tf_op jit(solution)/shard_map/reduce_scatter | solution.py:216
  756.4 2.0 multiply_reduce_fusion.12
  758.4 78.9 %all-reduce.13.cloned.1.call-done = f32[3,512,128]{2,0,1:T(4,128)} async-done(((f32[3,512,128]{2,0,1:T(4,128)}), f32[3,512,128]{2,0,1:T(4,128)}) %all-reduce.13.cloned.1.call-update) | async-done | bytes 786448
  837.3 0.9 constant_dynamic-slice_fusion
  838.3 1.3 multiply_reduce_fusion.10
  840.3 153.2 %all-reduce.15.cloned.1.call-done = (f32[2048,512]{1,0:T(8,128)}, f32[2048,512]{1,0:T(8,128)}) async-done(((f32[2048,512]{1,0:T(8,128)}, f32[2048,512]{1,0:T(8,128)}), (f32[2048,512]{1,0:T(8,128)}, f32[2048,512]{1,0:T(8,128)})) %all-reduce.15.cloned.1.call-update) | async-done | bytes 8388624 | tf_op jit(solution)/shard_map/psum | solution.py:147
  993.5 4.0 fusion.14
  998.5 5.5 fusion.13
  1004.0 55.9 %reduce-scatter.13.cloned.1.call-done = f32[64,4]{1,0:T(8,128)} async-done(((f32[512,4]{1,0:T(8,128)}), f32[64,4]{1,0:T(8,128)}) %reduce-scatter.13.cloned.1.call-update) | async-done | bytes 1040
  1060.8 1.2 multiply_reduce_fusion.14
  1062.0 3.3 stack.88
  1065.4 3.3 stack.101
  1068.8 5.5 add_convert_fusion
  1074.3 40.1 %all-reduce.2 = (f32[5]{0:T(128)S(1)}, f32[5]{0:T(128)S(1)}) all-reduce(f32[5]{0:T(128)S(1)} %pad_multiply_fusion, f32[5]{0:T(128)S(1)} %pad_multiply_fusion.1), channel_id=1, replica_groups=mesh['seq'=8,'head'=4] {'seq','head'}, use_global_device_ids=true, to_apply=%region_38.39 | all-reduce | flops 10 | bytes 80 | tf_op jit(solution)/shard_map/psum | solution.py:238
  (175 shorter events, 15.4 us)
Async XLA Ops:
  7.2 59.5 %copy-start.3 = (bf16[2048,512]{1,0:T(8,128)(2,1)S(1)}, bf16[2048,512]{1,0:T(8,128)(2,1)}, u32[]{:S(2)}) copy-start(bf16[2048,512]{1,0:T(8,128)(2,1)} %param.18) | copy-start | bytes 6291460
  7.2 27.7 %copy-start.22 = (f32[3,64,128]{2,1,0:T(8,128)S(1)}, f32[3,64,128]{2,1,0:T(8,128)}, u32[]{:S(2)}) copy-start(f32[3,64,128]{2,1,0:T(8,128)} %param.21) | copy-start | bytes 294916
  7.2 288.6 %all-reduce.9.cloned.1.call-start = ((), (), s32[]{:S(2)}) async-start(), calls=%async_computation.4 | async-start | bytes 8388608 | tf_op jit(solution)/shard_map/psum | solution.py:141
  30.4 36.3 %copy-start.47 = (f32[1,512]{1,0:T(1,128)}, f32[1,512]{1,0:T(1,128)S(1)}, u32[]{:S(2)}) copy-start(f32[1,512]{1,0:T(1,128)S(1)} %get-tuple-element.222) | copy-start | bytes 6148
  30.5 36.3 %copy-start.55 = (f32[1,512]{1,0:T(1,128)}, f32[1,512]{1,0:T(1,128)S(1)}, u32[]{:S(2)}) copy-start(f32[1,512]{1,0:T(1,128)S(1)} %get-tuple-element.221) | copy-start | bytes 6148
  32.4 36.2 %copy-start.35 = (f32[2048]{0:T(1024)}, f32[2048]{0:T(1024)S(1)}, u32[]{:S(2)}) copy-start(f32[2048]{0:T(1024)S(1)} %broadcast_multiply_fusion.9) | copy-start | bytes 24580
  34.9 33.7 %copy-start.42 = (f32[2048]{0:T(1024)}, f32[2048]{0:T(1024)S(1)}, u32[]{:S(2)}) copy-start(f32[2048]{0:T(1024)S(1)} %add_rsqrt_fusion.1) | copy-start | bytes 24580
  66.7 2.0 copy-start.29
  66.7 5.5 copy-start.57
  69.9 15.9 %copy-start.15 = (bf16[2,2048,128]{1,2,0:T(8,128)(2,1)}, bf16[2,2048,128]{1,2,0:T(8,128)(2,1)S(1)}, u32[]{:S(2)}) copy-start(bf16[2,2048,128]{1,2,0:T(8,128)(2,1)S(1)} %stack.106) | copy-start | bytes 3145732
  69.9 54.7 %collective-permute-start = (bf16[2,2048,128]{1,2,0:T(8,128)(2,1)S(1)}, bf16[2,2048,128]{1,2,0:T(8,128)(2,1)}, u32[]{:S(2)}, u32[]{:S(2)}) collective-permute-start(bf16[2,2048,128]{1,2,0:T(8,128)(2,1)S(1)} %stack.106), channel_id=1, source_target_pairs={{0,4},{4,8},{8,12},{12,16},{16,20},{20,24},{24,28},{1,5},{5,9},{9,... | collective-permute-start | bytes 3145736 | tf_op jit(solution)/shard_map/ppermute | solution.py:24
  72.8 14.1 %copy-start.33 = (f32[128,64]{0,1:T(8,128)S(1)}, f32[128,64]{0,1:T(8,128)}, u32[]{:S(2)}) copy-start(f32[128,64]{0,1:T(8,128)} %param.24) | copy-start | bytes 98308
  86.9 68.1 %copy-start.10 = (bf16[1,2048,128]{1,2,0:T(8,128)(2,1)}, bf16[1,2048,128]{1,2,0:T(8,128)(2,1)S(1)}, u32[]{:S(2)}) copy-start(bf16[1,2048,128]{1,2,0:T(8,128)(2,1)S(1)} %slice.76) | copy-start | bytes 1572868
  126.3 28.8 %copy-start.7 = (bf16[1,4096,128]{1,2,0:T(8,128)(2,1)}, bf16[1,4096,128]{1,2,0:T(8,128)(2,1)S(1)}, u32[]{:S(2)}) copy-start(bf16[1,4096,128]{1,2,0:T(8,128)(2,1)S(1)} %get-tuple-element.208) | copy-start | bytes 3145732
  126.3 52.9 %copy-start.13 = (bf16[1,4096,128]{1,2,0:T(8,128)(2,1)}, bf16[1,4096,128]{1,2,0:T(8,128)(2,1)S(1)}, u32[]{:S(2)}) copy-start(bf16[1,4096,128]{1,2,0:T(8,128)(2,1)S(1)} %get-tuple-element.209) | copy-start | bytes 3145732
  207.9 2.8 copy-start.20
  210.6 159.8 %reduce-scatter.11.cloned.1.call-start = ((), (), s32[]{:S(2)}) async-start(), calls=%async_computation.8 | async-start | bytes 1179648 | tf_op jit(solution)/shard_map/reduce_scatter | solution.py:218
  300.5 3.3 copy-start.18
  301.7 2.0 copy-start.9
  303.7 66.7 %copy-start.26 = (f32[512,64]{0,1:T(8,128)S(1)}, f32[512,64]{0,1:T(8,128)}, u32[]{:S(2)}) copy-start(f32[512,64]{0,1:T(8,128)} %param.30) | copy-start | bytes 393220
  303.7 66.7 %copy-start.37 = (f32[512,64]{0,1:T(8,128)S(1)}, f32[512,64]{0,1:T(8,128)}, u32[]{:S(2)}) copy-start(f32[512,64]{0,1:T(8,128)} %param.31) | copy-start | bytes 393220
  303.8 66.7 %copy-start.38 = (f32[512,64]{0,1:T(8,128)S(1)}, f32[512,64]{0,1:T(8,128)}, u32[]{:S(2)}) copy-start(f32[512,64]{0,1:T(8,128)} %param.32) | copy-start | bytes 393220
  306.6 192.4 %all-reduce.11.cloned.1.call-start = ((), (), s32[]{:S(2)}) async-start(), calls=%async_computation.5 | async-start | bytes 8388608 | tf_op jit(solution)/shard_map/psum | solution.py:154
  404.3 5.7 copy-start.24
  414.5 325.8 %reduce-scatter.9.cloned.1.call-start = ((), (), s32[]{:S(2)}) async-start(), calls=%async_computation.7 | async-start | bytes 1179648 | tf_op jit(solution)/shard_map/reduce_scatter | solution.py:217
  418.5 337.9 %reduce-scatter.7.cloned.1.call-start = ((), (), s32[]{:S(2)}) async-start(), calls=%async_computation.6 | async-start | bytes 294912 | tf_op jit(solution)/shard_map/reduce_scatter | solution.py:216
  499.0 5.5 copy-start.1
  499.0 5.9 copy-start.6
  508.4 1.9 copy-start.2
  511.2 29.7 %copy-start.14 = (bf16[1,4096,128]{1,2,0:T(8,128)(2,1)S(1)}, bf16[1,4096,128]{1,2,0:T(8,128)(2,1)}, u32[]{:S(2)}) copy-start(bf16[1,4096,128]{1,2,0:T(8,128)(2,1)} %copy-done.13) | copy-start | bytes 3145732
  593.5 74.1 %copy-start.5 = (f32[1,4096,128]{2,1,0:T(8,128)}, f32[1,4096,128]{2,1,0:T(8,128)S(1)}, u32[]{:S(2)}) copy-start(f32[1,4096,128]{2,1,0:T(8,128)S(1)} %copy.110) | copy-start | bytes 6291460
  593.5 56.0 %copy-start.11 = (bf16[1,2048,128]{1,2,0:T(8,128)(2,1)S(1)}, bf16[1,2048,128]{1,2,0:T(8,128)(2,1)}, u32[]{:S(2)}) copy-start(bf16[1,2048,128]{1,2,0:T(8,128)(2,1)} %copy-done.10) | copy-start | bytes 1572868
  667.7 4.2 copy-start.8
  670.4 18.0 %copy-start.17 = (bf16[2,64,2048]{2,1,0:T(8,128)(2,1)S(1)}, bf16[2,64,2048]{2,1,0:T(8,128)(2,1)}, u32[]{:S(2)}) copy-start(bf16[2,64,2048]{2,1,0:T(8,128)(2,1)} %copy-done.16) | copy-start | bytes 1572868
  670.4 50.3 %collective-permute-start.1 = (f32[2,2048,128]{2,1,0:T(8,128)}, f32[2,2048,128]{2,1,0:T(8,128)}, u32[]{:S(2)}, u32[]{:S(2)}) collective-permute-start(f32[2,2048,128]{2,1,0:T(8,128)} %pad_maximum_fusion), channel_id=1, source_target_pairs={{4,0},{8,4},{12,8},{16,12},{20,16},{24,20},{28,24},{5,1},{9,5},{13... | collective-permute-start | bytes 6291464 | tf_op jit(solution)/shard_map/ppermute | solution.py:24
  692.2 30.9 %copy-start.4 = (bf16[2048,512]{1,0:T(8,128)(2,1)S(1)}, bf16[2048,512]{1,0:T(8,128)(2,1)}, u32[]{:S(2)}) copy-start(bf16[2048,512]{1,0:T(8,128)(2,1)} %param.18) | copy-start | bytes 6291460
  692.2 30.9 %copy-start.36 = (f32[2048]{0:T(1024)S(1)}, f32[2048]{0:T(1024)}, u32[]{:S(2)}) copy-start(f32[2048]{0:T(1024)} %copy-done.35) | copy-start | bytes 24580
  692.2 30.9 %copy-start.43 = (f32[2048]{0:T(1024)S(1)}, f32[2048]{0:T(1024)}, u32[]{:S(2)}) copy-start(f32[2048]{0:T(1024)} %copy-done.42) | copy-start | bytes 24580
  692.2 30.9 %copy-start.48 = (f32[1,512]{1,0:T(1,128)S(1)}, f32[1,512]{1,0:T(1,128)}, u32[]{:S(2)}) copy-start(f32[1,512]{1,0:T(1,128)} %copy-done.47) | copy-start | bytes 6148
  692.2 30.9 %copy-start.56 = (f32[1,512]{1,0:T(1,128)S(1)}, f32[1,512]{1,0:T(1,128)}, u32[]{:S(2)}) copy-start(f32[1,512]{1,0:T(1,128)} %copy-done.55) | copy-start | bytes 6148
  692.3 145.1 %all-reduce.13.cloned.1.call-start = ((), (), s32[]{:S(2)}) async-start(), calls=%async_computation.10 | async-start | bytes 2097152
  729.1 6.0 copy-start.30
  729.1 264.4 %all-reduce.15.cloned.1.call-start = ((), (), s32[]{:S(2)}) async-start(), calls=%async_computation.11 | async-start | bytes 16777216 | tf_op jit(solution)/shard_map/psum | solution.py:147
  729.2 5.9 copy-start.25
  738.4 2.0 copy-start.21
  738.4 2.0 copy-start.39
  738.4 2.0 copy-start.40
  738.4 18.0 %copy-start.34 = (f32[128,64]{0,1:T(8,128)S(1)}, f32[128,64]{0,1:T(8,128)}, u32[]{:S(2)}) copy-start(f32[128,64]{0,1:T(8,128)} %param.24) | copy-start | bytes 98308
  738.4 18.0 %copy-start.44 = (f32[128,64]{0,1:T(8,128)S(1)}, f32[128,64]{0,1:T(8,128)}, u32[]{:S(2)}) copy-start(f32[128,64]{0,1:T(8,128)} %param.25) | copy-start | bytes 98308
  738.4 17.9 %copy-start.45 = (f32[128,64]{0,1:T(8,128)S(1)}, f32[128,64]{0,1:T(8,128)}, u32[]{:S(2)}) copy-start(f32[128,64]{0,1:T(8,128)} %param.26) | copy-start | bytes 98308
  738.5 99.8 %copy-start.23 = (f32[3,64,128]{2,1,0:T(8,128)S(1)}, f32[3,64,128]{2,1,0:T(8,128)}, u32[]{:S(2)}) copy-start(f32[3,64,128]{2,1,0:T(8,128)} %param.21) | copy-start | bytes 294916
  738.5 99.8 %copy-start.31 = (f32[3,64,128]{2,1,0:T(8,128)S(1)}, f32[3,64,128]{2,1,0:T(8,128)}, u32[]{:S(2)}) copy-start(f32[3,64,128]{2,1,0:T(8,128)} %param.22) | copy-start | bytes 294916
  738.5 99.8 %copy-start.41 = (f32[3,64,128]{2,1,0:T(8,128)S(1)}, f32[3,64,128]{2,1,0:T(8,128)}, u32[]{:S(2)}) copy-start(f32[3,64,128]{2,1,0:T(8,128)} %param.23) | copy-start | bytes 294916
  738.5 255.0 %copy-start.49 = (f32[1,512]{1,0:T(1,128)S(1)}, f32[1,512]{1,0:T(1,128)}, u32[]{:S(2)}) copy-start(f32[1,512]{1,0:T(1,128)} %copy-done.47) | copy-start | bytes 6148
  738.5 321.4 %reduce-scatter.13.cloned.1.call-start = ((), (), s32[]{:S(2)}) async-start(), calls=%async_computation.9 | async-start | bytes 294912
  740.3 257.3 %copy-start.50 = (f32[512]{0:T(512)S(1)}, f32[512]{0:T(512)}, u32[]{:S(2)}) copy-start(f32[512]{0:T(512)} %get-tuple-element.168) | copy-start | bytes 6148
  740.3 257.3 %copy-start.51 = (f32[512]{0:T(512)S(1)}, f32[512]{0:T(512)}, u32[]{:S(2)}) copy-start(f32[512]{0:T(512)} %get-tuple-element.175) | copy-start | bytes 6148
  839.6 164.5 %copy-start.32 = (f32[3,64,128]{2,1,0:T(8,128)}, f32[3,64,128]{2,1,0:T(8,128)S(1)}, u32[]{:S(2)}) copy-start(f32[3,64,128]{2,1,0:T(8,128)S(1)} %get-tuple-element.205) | copy-start | bytes 294916
  998.5 62.3 %copy-start.46 = (f32[4,64]{1,0:T(4,128)S(1)}, f32[4,64]{1,0:T(4,128)}, u32[]{:S(2)}) copy-start(f32[4,64]{1,0:T(4,128)} %param.33) | copy-start | bytes 3076
  998.5 62.3 %copy-start.53 = (f32[4,64]{1,0:T(4,128)S(1)}, f32[4,64]{1,0:T(4,128)}, u32[]{:S(2)}) copy-start(f32[4,64]{1,0:T(4,128)} %param.34) | copy-start | bytes 3076
  998.5 62.3 %copy-start.54 = (f32[4,64]{1,0:T(4,128)S(1)}, f32[4,64]{1,0:T(4,128)}, u32[]{:S(2)}) copy-start(f32[4,64]{1,0:T(4,128)} %param.35) | copy-start | bytes 3076
  1060.8 13.5 %copy-start.52 = (f32[4,64]{1,0:T(4,128)}, f32[4,64]{1,0:T(4,128)S(1)}, u32[]{:S(2)}) copy-start(f32[4,64]{1,0:T(4,128)S(1)} %copy.120) | copy-start | bytes 3076
  1068.8 51.9 %copy-start.27 = (f32[512,64]{0,1:T(8,128)S(1)}, f32[512,64]{0,1:T(8,128)}, u32[]{:S(2)}) copy-start(f32[512,64]{0,1:T(8,128)} %param.30) | copy-start | bytes 393220
  1068.8 51.9 %copy-start.28 = (f32[512,64]{0,1:T(8,128)S(1)}, f32[512,64]{0,1:T(8,128)}, u32[]{:S(2)}) copy-start(f32[512,64]{0,1:T(8,128)} %get-tuple-element.194) | copy-start | bytes 393220
  (5 other events, 5.8 us)
Sparse Core Ops, SparseCore 0:
  210.8 85.0 all-reduce.8
  306.8 63.6 reduce-scatter.10
  414.7 84.3 all-reduce.10
  503.2 63.6 reduce-scatter.8
  692.4 63.9 reduce-scatter.6
  760.3 76.9 all-reduce.12
  840.6 152.8 all-reduce.14
  998.6 61.2 reduce-scatter.12
where the time goes:
time: 1130 us
  waiting for transfers between devices  528 us (47%)
  matrix products  207 us (18%)
  blocking collectives  194 us (17%)
  other arithmetic  149 us (13%)
  local copies, waits for them, and re-layouts  28.5 us (3%)
  between operations  19.1 us (2%)
    psum x1, waiting for transfers between devices, local(): lax.psum(jnp.dot(active_low, full_down, preferred_element_type=jnp.float3...  153 us
    unnamed x10, waiting for transfers between devices  135 us
    psum x1, waiting for transfers between devices, local(): lax.psum(jnp.dot(grad_upper, full_up.T, preferred_element_type=jnp.float3...  80 us
    reduce_scatter x1, waiting for transfers between devices, local(): lax.psum_scatter(grad_down, 'seq', scatter_dimension=1, tiled=True)  63.7 us
    convert_element_type x1, other arithmetic, local(): (probability * (grad_prob - delta[..., None])).astype(jnp.bfloat16)  56 us
    psum x1, waiting for transfers between devices, local(): lax.psum(jnp.dot(attended_low, full_out, preferred_element_type=jnp.float...  53.7 us
    dot_general x1, matrix products, local(): jnp.einsum('qhd,khd->hqk', grad_att_heads, value_heads, preferred_element...  50.7 us
    psum x1, blocking collectives, local(): lax.psum((squares_of(masters, head_first), squares_of(directions, head_fi...  40.1 us
  transfers between devices with their start and end apart: 10, of which 8 were waited for; matrix products, arithmetic and copies ran while one was open for 21% of the time, Pallas kernels for 0%

commit v1 on v0

v1 whole, which is shorter than its diff:
```python
import functools

import jax
import jax.numpy as jnp
from jax import lax
from jax.experimental import pallas as pl
from jax.experimental.pallas import tpu as pltpu
from jax.sharding import PartitionSpec as P

HEAD_DIM = 64
FRAME_TOKENS = 64
MOST_FRAMES = 16
STEP = 5

EPS_NORM = 1e-05
BETA_ONE = 0.5
BETA_TWO = 0.6
RATE = 0.3
DECAY = 0.01
EPS_ADAM = 1e-06
MASKED = -1e30

MESH = pl.DeviceIdType.MESH
F32 = jnp.float32
BF16 = jnp.bfloat16
TILE = 128
KEYS = MOST_FRAMES * FRAME_TOKENS + TILE
ROWS = 64

DOWN, UP, OUT, QKV = range(4)


def nn(a, b):
    return lax.dot_general(a, b, (((1,), (0,)), ((), ())), preferred_element_type=F32)


def nt(a, b):
    return lax.dot_general(a, b, (((1,), (1,)), ((), ())), preferred_element_type=F32)


def tn(a, b):
    return lax.dot_general(a, b, (((0,), (0,)), ((), ())), preferred_element_type=F32)


def normalize(values):
    average = jnp.mean(values, axis=-1, keepdims=True)
    centered = values - average
    variance = jnp.mean(centered * centered, axis=-1, keepdims=True)
    inverse = lax.rsqrt(variance + EPS_NORM)
    return centered * inverse, inverse


def norm_back(gradient, normed, inverse, gain_row):
    scaled = gradient * gain_row
    return inverse * (
        scaled
        - jnp.mean(scaled, axis=-1, keepdims=True)
        - normed * jnp.mean(scaled * normed, axis=-1, keepdims=True)
    )


def gelu_both(inner):
    root = 0.7978845608028654
    cube = 0.044715
    square = inner * inner
    curved = jnp.tanh(root * inner * (1.0 + cube * square))
    half = 0.5 * (1.0 + curved)
    value = inner * half
    slope = half + 0.5 * inner * (1.0 - curved * curved) * (root * (1.0 + 3.0 * cube * square))
    return value, slope


def lamb_direction(master, moment, square, gradient):
    new_first = BETA_ONE * moment + (1.0 - BETA_ONE) * gradient
    new_second = BETA_TWO * square + (1.0 - BETA_TWO) * gradient * gradient
    direction = (
        new_first
        / (1.0 - BETA_ONE**STEP)
        / (jnp.sqrt(new_second / (1.0 - BETA_TWO**STEP)) + EPS_ADAM)
        + DECAY * master
    )
    return new_first, new_second, direction


def flat(block):
    pieces, rows, columns = block.shape
    if rows % 16:
        block = block.astype(F32)
    return block.reshape(pieces * rows, columns).astype(BF16)


def cut(matrix, pieces):
    rows, columns = matrix.shape
    return matrix.reshape(pieces, rows // pieces, columns).astype(BF16)


def layer_kernel(
    seq_count,
    head_count,
    tok,
    cot,
    frames,
    qkv_w,
    out_w,
    up_w,
    down_w,
    norm_w,
    qkv_m,
    qkv_u,
    out_m,
    out_u,
    up_m,
    up_u,
    down_m,
    down_u,
    norm_m,
    norm_u,
    block_out,
    input_grad,
    qkv_g,
    out_g,
    up_g,
    down_g,
    norm_g,
    squares,
    w_qkv,
    w_out,
    w_up,
    w_down,
    norm_parts,
    norm_full,
    ext,
    cot_own,
    h1,
    h1_t,
    q_all,
    k_all,
    v_all,
    prob,
    attended,
    resid,
    h2,
    h2_t,
    cot_t,
    mlp,
    dh2,
    wide_a,
    wide_b,
    act,
    dup,
    low_out,
    dr_low,
    d_att,
    dk_acc,
    dv_acc,
    dq_all,
    dk_all,
    dv_all,
    dh1,
    halo_low,
    halo_in,
    g_down,
    g_up,
    g_out,
    g_qkv,
    c_down,
    c_up,
    c_out,
    c_qkv,
    x_down,
    x_up,
    x_out,
    x_qkv,
    s_down,
    s_up,
    s_out,
    s_qkv,
    norm_sum,
    norm_c,
    norm_x,
    norm_s,
    sq_c,
    sq_x,
    sq_s,
    loc_sem,
    halo_sem,
    normp_sem,
    ags_send,
    ags_recv,
    agx_sem,
    agc_sem,
    rsc_sem,
    rsx_sem,
    rss_send,
    rss_recv,
    small_sem,
    norm_s_send,
    norm_s_recv,
    sq_s_send,
    sq_s_recv,
    out_sem,
    back_sem,
):
    S, H = seq_count, head_count
    T = cot_own.shape[0]
    R = qkv_w.shape[1]
    s = lax.axis_index("seq")
    h = lax.axis_index("head")
    hx = lax.div(h, 2)
    hc = lax.rem(h, 2)
    other_core = (s, h + 1 - 2 * hc)
    other_x = (s, lax.rem(h + 2, H))
    mine = hc * 2 + hx
    near = hc * 2 + 1 - hx
    mine_pair = hc * 2
    other_pair = (1 - hc) * 2
    total = S * H
    place = s * H + h

    def device_at(number):
        number = lax.rem(number + total, total)
        return (lax.div(number, H), lax.rem(number, H))

    def seq_peer(i):
        return lax.rem(s + i, S)

    def remote(src, dst, send, recv, device):
        return pltpu.make_async_remote_copy(
            src_ref=src, dst_ref=dst, send_sem=send, recv_sem=recv, device_id=device, device_id_type=MESH
        )

    def rows_of(index, count):
        return pl.ds(pl.multiple_of(index * count, count), count)

    cot_copy = pltpu.make_async_copy(cot.at[rows_of(h, T)], cot_own, loc_sem.at[3])
    cot_copy.start()

    def ext_copy(chunk):
        return pltpu.make_async_copy(
            tok.at[rows_of(jnp.maximum(h - 2 + chunk, 0), T)], ext.at[pl.ds(chunk * T, T)], loc_sem.at[chunk]
        )

    for chunk in range(3):

        @pl.when(h - 2 + chunk >= 0)
        def _():
            ext_copy(chunk).start()

    for t in range(3):
        w_qkv[mine, s, :, t * 128 : (t + 1) * 128] = qkv_w[t].astype(BF16)
    w_out[mine, s] = out_w[...].astype(BF16)
    w_up[mine, s] = up_w[...].astype(BF16)
    w_down[mine, s] = down_w[...].astype(BF16)
    norm_full[...] = jnp.zeros_like(norm_full)
    norm_full[0:4, 0:R] = norm_w[...].astype(BF16).astype(F32)
    norm_parts[s] = pltpu.roll(norm_full[...], s * R, axis=1)

    barrier = pltpu.get_barrier_semaphore()

    def greet(i, carry):
        pl.semaphore_signal(barrier, inc=1, device_id=(seq_peer(i), h), device_id_type=MESH)
        return carry

    lax.fori_loop(1, S, greet, 0)
    for device in (other_core, other_x, device_at(place + 1), device_at(place + 2)):
        pl.semaphore_signal(barrier, inc=1, device_id=device, device_id_type=MESH)
    pl.semaphore_wait(barrier, S - 1 + 4)

    kinds_w = {DOWN: w_down, UP: w_up, OUT: w_out, QKV: w_qkv}

    def gather_seq(kind, i):
        buffer = kinds_w[kind]
        return remote(
            buffer.at[mine, s], buffer.at[mine, s], ags_send.at[kind, i], ags_recv.at[kind, s], (seq_peer(i), h)
        )

    def gather_seq_start(kind):
        def one(i, carry):
            gather_seq(kind, i).start()
            return carry

        lax.fori_loop(1, S, one, 0)

    def gather_seq_wait(kind):
        buffer = kinds_w[kind]

        def one(i, carry):
            peer = seq_peer(i)
            remote(
                buffer.at[mine, peer],
                buffer.at[mine, peer],
                ags_send.at[kind, i],
                ags_recv.at[kind, peer],
                (peer, h),
            ).wait_recv()
            return carry

        lax.fori_loop(1, S, one, 0)

    def gather_x(kind, group):
        buffer = kinds_w[kind]
        return remote(buffer.at[group], buffer.at[group], agx_sem.at[0, kind], agx_sem.at[1, kind], other_x)

    def gather_core(kind, pair):
        buffer = kinds_w[kind]
        return remote(
            buffer.at[pl.ds(pair, 2)],
            buffer.at[pl.ds(pair, 2)],
            agc_sem.at[0, kind],
            agc_sem.at[1, kind],
            other_core,
        )

    def norm_part(i):
        return remote(
            norm_parts.at[s], norm_parts.at[s], normp_sem.at[0, i], normp_sem.at[1, s], (seq_peer(i), h)
        )

    def norm_part_start(i, carry):
        norm_part(i).start()
        return carry

    lax.fori_loop(1, S, norm_part_start, 0)
    gather_seq_start(QKV)

    def halo_copy(chunk):
        return remote(
            tok.at[rows_of(jnp.minimum(h - 2 + chunk + H, H - 1), T)],
            ext.at[pl.ds(chunk * T, T)],
            halo_sem.at[0, chunk],
            halo_sem.at[1, chunk],
            (seq_peer(1), h),
        )

    for chunk in range(2):

        @pl.when(h - 2 + chunk < 0)
        def _():
            halo_copy(chunk).start()

    for kind in (OUT, UP, DOWN):
        gather_seq_start(kind)

    first_frame = place * (T // FRAME_TOKENS)
    own_frames = T // FRAME_TOKENS

    def clip_step(c, carry):
        end, lows = carry
        start = end
        end = start + frames[c]
        lows = tuple(
            jnp.where((start <= first_frame + f) & (first_frame + f < end), start, lows[f])
            for f in range(own_frames)
        )
        return end, lows

    _, clip_low = lax.fori_loop(
        0, frames.shape[0], clip_step, (jnp.int32(0), tuple(jnp.int32(0) for _ in range(own_frames)))
    )

    def norm_part_wait(i, carry):
        peer = seq_peer(i)
        remote(
            norm_parts.at[peer], norm_parts.at[peer], normp_sem.at[0, i], normp_sem.at[1, peer], (peer, h)
        ).wait_recv()
        return carry

    lax.fori_loop(1, S, norm_part_wait, 0)
    norm_full[...] = lax.fori_loop(
        0, S, lambda i, carry: carry + norm_parts[i], jnp.zeros(norm_full.shape, F32)
    )

    for chunk in range(3):

        @pl.when(h - 2 + chunk >= 0)
        def _():
            ext_copy(chunk).wait()

        if chunk < 2:

            @pl.when(h - 2 + chunk < 0)
            def _():
                halo_copy(chunk).wait_recv()

    gain_one, shift_one = norm_full[0:1, :], norm_full[1:2, :]
    gain_two, shift_two = norm_full[2:3, :], norm_full[3:4, :]

    def first_norm(b, carry):
        at = rows_of(b, ROWS)
        normed, _ = normalize(ext[at, :].astype(F32))
        h1[at, :] = (normed * gain_one + shift_one).astype(BF16)
        return carry

    lax.fori_loop(0, 3 * T // ROWS, first_norm, 0)

    gather_seq_wait(QKV)
    gather_x(QKV, mine).start()
    gather_x(QKV, near).wait_recv()
    gather_core(QKV, mine_pair).start()
    for chunk in range(3):
        h1_t[:, chunk * T : (chunk + 1) * T] = h1[chunk * T : (chunk + 1) * T, :].T
    cot_copy.wait()
    cot_t[...] = cot_own[...].T
    gather_core(QKV, other_pair).wait_recv()

    def project(p, carry):
        weight = flat(w_qkv[p])
        for chunk in range(3):
            at = pl.ds(chunk * T, T)
            if chunk == 2:
                out = nn(h1[at, :], weight)
                q_all[p] = out[:, 0:128].astype(BF16) * jnp.asarray(HEAD_DIM**-0.5, BF16)
                out = out[:, 128:384]
            else:
                out = nn(h1[at, :], weight[:, 128:384])
            k_all[p, at, :] = out[:, 0:128].astype(BF16)
            v_all[p, at, :] = out[:, 128:256].astype(BF16)
        return carry

    lax.fori_loop(0, H, project, 0)

    lane = lax.broadcasted_iota(jnp.int32, (1, 128), 1)
    first_head = jnp.where(lane < HEAD_DIM, 1.0, 0.0).astype(BF16)
    second_head = jnp.where(lane < HEAD_DIM, 0.0, 1.0).astype(BF16)
    feature = lax.broadcasted_iota(jnp.int32, (128, TILE), 0)

    def two_heads(block):
        return jnp.concatenate([block * first_head, block * second_head], axis=0)

    def own_halves(block):
        return jnp.where(feature < HEAD_DIM, block[:, 0:TILE], block[:, TILE : 2 * TILE])

    key_frames = KEYS // FRAME_TOKENS

    def bias_of(i):
        query_lane = lax.broadcasted_iota(jnp.int32, (key_frames, 1, 2 * TILE), 2)
        later = lax.rem(query_lane, TILE) >= FRAME_TOKENS
        low = jnp.where(later, clip_low[2 * i + 1], clip_low[2 * i])
        high = first_frame + 2 * i + later.astype(jnp.int32)
        key_frame = (
            first_frame
            - MOST_FRAMES
            + 2 * i
            + lax.broadcasted_iota(jnp.int32, (key_frames, 1, 2 * TILE), 0)
        )
        return jnp.where((key_frame >= low) & (key_frame <= high), 0.0, MASKED).astype(F32)

    biases = [bias_of(i) for i in range(T // TILE)]

    def attend(p, carry):
        for i in range(T // TILE):
            own = pl.ds(i * TILE, TILE)
            window = pl.ds(i * TILE, KEYS)
            queries = two_heads(q_all[p, own, :])
            scores = nt(k_all[p, window, :], queries)
            scores = (scores.reshape(key_frames, FRAME_TOKENS, 2 * TILE) + biases[i]).reshape(KEYS, 2 * TILE)
            highest = jnp.max(scores, axis=0, keepdims=True)
            powers = jnp.exp(scores - highest)
            inverse = 1.0 / jnp.sum(powers, axis=0, keepdims=True)
            low = (powers * inverse).astype(BF16)
            prob[p, i] = low
            mixed = own_halves(tn(v_all[p, window, :], low))
            attended[p, own, :] = mixed.T.astype(BF16)
        return carry

    lax.fori_loop(0, 1, attend, 0)
    gather_seq_wait(OUT)
    gather_x(OUT, mine).start()
    lax.fori_loop(1, 2, attend, 0)
    gather_x(OUT, near).wait_recv()
    gather_core(OUT, mine_pair).start()
    gather_seq_wait(UP)
    gather_x(UP, mine).start()
    lax.fori_loop(2, 3, attend, 0)
    gather_seq_wait(DOWN)
    gather_x(DOWN, mine).start()
    lax.fori_loop(3, 4, attend, 0)
    gather_x(UP, near).wait_recv()
    gather_core(UP, mine_pair).start()
    gather_core(OUT, other_pair).wait_recv()

    acc = nt(attended[0], flat(w_out[0]))
    for p in range(1, H):
        acc = acc + nt(attended[p], flat(w_out[p]))
    resid[...] = acc

    def second_norm(b, carry):
        at = rows_of(b, ROWS)
        whole = ext[pl.ds(pl.multiple_of(2 * T + b * ROWS, ROWS), ROWS), :].astype(F32) + resid[at, :]
        resid[at, :] = whole
        normed, _ = normalize(whole)
        h2[at, :] = (normed * gain_two + shift_two).astype(BF16)
        return carry

    lax.fori_loop(0, T // ROWS, second_norm, 0)
    h2_t[...] = h2[...].T
    gather_x(DOWN, near).wait_recv()
    gather_core(DOWN, mine_pair).start()
    gather_core(UP, other_pair).wait_recv()
    gather_core(DOWN, other_pair).wait_recv()

    mlp[...] = jnp.zeros_like(mlp)
    dh2[...] = jnp.zeros_like(dh2)

    def hidden(c, carry):
        up_block = flat(w_up[c])
        down_block = flat(w_down[c])
        wide_a[...] = nn(h2[...], up_block)
        wide_b[...] = nn(cot_own[...], down_block)

        def pointwise(b, inner):
            at = rows_of(b, ROWS)
            value, slope = gelu_both(wide_a[at, :])
            act[at, :] = value.astype(BF16)
            dup[at, :] = (wide_b[at, :] * slope).astype(BF16)
            return inner

        lax.fori_loop(0, T // ROWS, pointwise, 0)
        mlp[...] += nt(act[...], down_block)
        dh2[...] += nt(dup[...], up_block)
        g_down[c] = cut(nn(cot_t[...], act[...]), S)
        g_up[c] = cut(nn(h2_t[...], dup[...]), S)
        return carry

    lax.fori_loop(0, H, hidden, 0)

    grads = {DOWN: g_down, UP: g_up, OUT: g_out, QKV: g_qkv}
    from_core = {DOWN: c_down, UP: c_up, OUT: c_out, QKV: c_qkv}
    from_x = {DOWN: x_down, UP: x_up, OUT: x_out, QKV: x_qkv}
    from_seq = {DOWN: s_down, UP: s_up, OUT: s_out, QKV: s_qkv}

    def scatter_core(kind):
        return remote(
            grads[kind].at[pl.ds(other_pair, 2)],
            from_core[kind],
            rsc_sem.at[0, kind],
            rsc_sem.at[1, kind],
            other_core,
        )

    def scatter_core_sum(kind):
        scatter_core(kind).wait_recv()
        for gx in range(2):
            group = mine_pair + gx

            def add(b, carry):
                grads[kind][group, b] = (
                    grads[kind][group, b].astype(F32) + from_core[kind][gx, b].astype(F32)
                ).astype(BF16)
                return carry

            lax.fori_loop(0, S, add, 0)

    def scatter_x(kind):
        return remote(
            grads[kind].at[near], from_x[kind], rsx_sem.at[0, kind], rsx_sem.at[1, kind], other_x
        )

    def scatter_x_sum(kind):
        scatter_x(kind).wait_recv()

        def add(b, carry):
            grads[kind][mine, b] = (
                grads[kind][mine, b].astype(F32) + from_x[kind][b].astype(F32)
            ).astype(BF16)
            return carry

        lax.fori_loop(0, S, add, 0)

    def scatter_seq(kind, i):
        peer = seq_peer(i)
        return remote(
            grads[kind].at[mine, peer],
            from_seq[kind].at[s],
            rss_send.at[kind, i],
            rss_recv.at[kind, s],
            (peer, h),
        )

    def scatter_seq_start(kind):
        def one(i, carry):
            scatter_seq(kind, i).start()
            return carry

        lax.fori_loop(1, S, one, 0)

    def scatter_seq_sum(kind):
        landed = from_seq[kind]

        def one(i, carry):
            peer = seq_peer(i)
            remote(
                grads[kind].at[mine, peer],
                landed.at[peer],
                rss_send.at[kind, i],
                rss_recv.at[kind, peer],
                (peer, h),
            ).wait_recv()
            return carry

        lax.fori_loop(1, S, one, 0)

        def add(i, carry):
            return carry + landed[seq_peer(i)].astype(F32)

        return lax.fori_loop(1, S, add, grads[kind][mine, s].astype(F32))

    scatter_core(DOWN).start()
    scatter_core(UP).start()

    def finish_rows(target, low, at_sem):
        def slab(head):
            return target.at[rows_of(head, T)]

        keep = pltpu.make_async_copy(low, slab(h), out_sem.at[at_sem, 0])
        to_x = remote(low, slab(h), out_sem.at[at_sem, 1], out_sem.at[at_sem, 2], other_x)
        to_core = remote(low, slab(h), out_sem.at[at_sem, 3], out_sem.at[at_sem, 4], other_core)
        near_head = other_x[1]
        passed = remote(
            slab(near_head), slab(near_head), out_sem.at[at_sem, 5], out_sem.at[at_sem, 6], other_core
        )
        return keep, to_x, to_core, passed

    def sum_out(b, carry):
        at = rows_of(b, ROWS)
        low_out[at, :] = (resid[at, :] + mlp[at, :]).astype(BF16)
        return carry

    lax.fori_loop(0, T // ROWS, sum_out, 0)
    out_copies = finish_rows(block_out, low_out, 0)
    for copy in out_copies[:3]:
        copy.start()

    def second_back(b, carry):
        gain_sum, shift_sum = carry
        at = rows_of(b, ROWS)
        normed, inverse = normalize(resid[at, :])
        grad = dh2[at, :]
        mixed = cot_own[at, :].astype(F32) + norm_back(grad, normed, inverse, gain_two)
        resid[at, :] = mixed
        dr_low[at, :] = mixed.astype(BF16)
        gain_sum = gain_sum + jnp.sum(grad * normed, axis=0, keepdims=True)
        shift_sum = shift_sum + jnp.sum(grad, axis=0, keepdims=True)
        return gain_sum, shift_sum

    zero_row = jnp.zeros((1, resid.shape[1]), F32)
    gain_two_grad, shift_two_grad = lax.fori_loop(0, T // ROWS, second_back, (zero_row, zero_row))

    h2_t[...] = dr_low[...].T
    for p in range(H):
        d_att[p] = nn(dr_low[...], flat(w_out[p])).astype(BF16)
        g_out[p] = cut(nn(h2_t[...], attended[p]), S)
    scatter_core(OUT).start()
    scatter_core_sum(DOWN)
    scatter_x(DOWN).start()
    scatter_core_sum(UP)
    scatter_x(UP).start()

    def attend_back(p, carry):
        dk_acc[...] = jnp.zeros_like(dk_acc)
        dv_acc[...] = jnp.zeros_like(dv_acc)
        for i in range(T // TILE):
            own = pl.ds(i * TILE, TILE)
            window = pl.ds(i * TILE, KEYS)
            grad = d_att[p, own, :]
            stacked = two_heads(grad)
            queries = two_heads(q_all[p, own, :])
            products = (grad.astype(F32) * attended[p, own, :].astype(F32)).T
            delta = jnp.concatenate(
                [
                    jnp.sum(products[0:HEAD_DIM], axis=0, keepdims=True),
                    jnp.sum(products[HEAD_DIM:128], axis=0, keepdims=True),
                ],
                axis=1,
            )
            keys = k_all[p, window, :]
            low = prob[p, i]
            d_prob = nt(v_all[p, window, :], stacked)
            d_scores = (low.astype(F32) * (d_prob - delta)).astype(BF16)
            dv_acc[window, :] += nn(low, stacked)
            dk_acc[window, :] += nn(d_scores, queries)
            mixed = own_halves(tn(keys, d_scores)) * (HEAD_DIM**-0.5)
            dq_all[p, own, :] = mixed.T.astype(BF16)
        dk_all[p] = dk_acc[...].astype(BF16)
        dv_all[p] = dv_acc[...].astype(BF16)
        columns = [
            nn(h1_t[:, 2 * T : 3 * T], dq_all[p]),
            nn(h1_t[...], dk_all[p]),
            nn(h1_t[...], dv_all[p]),
        ]
        g_qkv[p] = cut(jnp.concatenate(columns, axis=1), S)
        return carry

    lax.fori_loop(0, 1, attend_back, 0)
    scatter_core_sum(OUT)
    scatter_x(OUT).start()
    scatter_x_sum(DOWN)
    scatter_seq_start(DOWN)
    lax.fori_loop(1, 2, attend_back, 0)
    scatter_x_sum(UP)
    scatter_seq_start(UP)
    lax.fori_loop(2, 3, attend_back, 0)
    scatter_x_sum(OUT)
    scatter_seq_start(OUT)
    out_copies[1].wait_recv()
    out_copies[3].start()
    lax.fori_loop(3, 4, attend_back, 0)
    scatter_core(QKV).start()

    dh1[...] = jnp.zeros_like(dh1)

    def back_halo(p, carry):
        weight = flat(w_qkv[p])
        for chunk in range(2):
            at = pl.ds(chunk * T, T)
            dh1[at, :] += nt(dk_all[p, at, :], weight[:, 128:256]) + nt(dv_all[p, at, :], weight[:, 256:384])
        return carry

    lax.fori_loop(0, H, back_halo, 0)

    def round_halo(b, carry):
        at = rows_of(b, ROWS)
        halo_low[at, :] = dh1[at, :].astype(BF16)
        return carry

    lax.fori_loop(0, 2 * T // ROWS, round_halo, 0)

    def back_copy(chunk):
        return remote(
            halo_low.at[pl.ds(chunk * T, T)],
            halo_in.at[chunk],
            back_sem.at[0, chunk],
            back_sem.at[1, chunk],
            device_at(place - 2 + chunk),
        )

    for chunk in range(2):
        back_copy(chunk).start()
    scatter_core_sum(QKV)
    scatter_x(QKV).start()

    def back_own(p, carry):
        weight = flat(w_qkv[p])
        at = pl.ds(2 * T, T)
        dh1[at, :] += (
            nt(dq_all[p], weight[:, 0:128])
            + nt(dk_all[p, at, :], weight[:, 128:256])
            + nt(dv_all[p, at, :], weight[:, 256:384])
        )
        return carry

    lax.fori_loop(0, H, back_own, 0)

    def first_sums(b, carry):
        gain_sum, shift_sum = carry
        at = rows_of(b, ROWS)
        normed, _ = normalize(ext[at, :].astype(F32))
        grad = dh1[at, :]
        return (
            gain_sum + jnp.sum(grad * normed, axis=0, keepdims=True),
            shift_sum + jnp.sum(grad, axis=0, keepdims=True),
        )

    gain_one_grad, shift_one_grad = lax.fori_loop(0, 3 * T // ROWS, first_sums, (zero_row, zero_row))
    norm_sum[...] = jnp.concatenate(
        [gain_one_grad, shift_one_grad, gain_two_grad, shift_two_grad, jnp.zeros((4, zero_row.shape[1]), F32)],
        axis=0,
    )
    norm_to_core = remote(norm_sum, norm_c, small_sem.at[0], small_sem.at[1], other_core)
    norm_to_core.start()
    norm_to_core.wait()
    norm_sum[...] += norm_c[...]
    norm_to_x = remote(norm_sum, norm_x, small_sem.at[2], small_sem.at[3], other_x)
    norm_to_x.start()
    scatter_x_sum(QKV)
    scatter_seq_start(QKV)
    norm_to_x.wait()
    norm_sum[...] += norm_x[...]

    def norm_seq(i):
        return remote(
            norm_sum, norm_s.at[s], norm_s_send.at[i], norm_s_recv.at[s], (seq_peer(i), h)
        )

    def norm_seq_start(i, carry):
        norm_seq(i).start()
        return carry

    lax.fori_loop(1, S, norm_seq_start, 0)

    for chunk in range(2):
        back_copy(chunk).wait_recv()

    def first_back(b, carry):
        at = rows_of(b, ROWS)
        below = pl.ds(pl.multiple_of(2 * T + b * ROWS, ROWS), ROWS)
        normed, inverse = normalize(ext[below, :].astype(F32))
        grad = dh1[below, :] + halo_in[0, at, :].astype(F32) + halo_in[1, at, :].astype(F32)
        dr_low[at, :] = (resid[at, :] + norm_back(grad, normed, inverse, gain_one)).astype(BF16)
        return carry

    lax.fori_loop(0, T // ROWS, first_back, 0)
    grad_copies = finish_rows(input_grad, dr_low, 1)
    for copy in grad_copies[:3]:
        copy.start()

    down_total = scatter_seq_sum(DOWN)
    down_g[...] = down_total
    up_total = scatter_seq_sum(UP)
    up_g[...] = up_total
    out_total = scatter_seq_sum(OUT)
    out_g[...] = out_total

    def sums_of(master, moment, square, gradient):
        _, _, direction = lamb_direction(master, moment, square, gradient)
        return jnp.sum(master * master), jnp.sum(direction * direction)

    down_sums = sums_of(down_w[...], down_m[...], down_u[...], down_total)
    up_sums = sums_of(up_w[...], up_m[...], up_u[...], up_total)
    out_sums = sums_of(out_w[...], out_m[...], out_u[...], out_total)

    qkv_total = scatter_seq_sum(QKV)
    weight_sum, update_sum = jnp.float32(0.0), jnp.float32(0.0)
    for t in range(3):
        part = qkv_total[:, t * 128 : (t + 1) * 128]
        qkv_g[t] = part
        sums = sums_of(qkv_w[t], qkv_m[t], qkv_u[t], part)
        weight_sum, update_sum = weight_sum + sums[0], update_sum + sums[1]
    qkv_sums = (weight_sum, update_sum)

    def norm_seq_wait(i, carry):
        peer = seq_peer(i)
        remote(norm_sum, norm_s.at[peer], norm_s_send.at[i], norm_s_recv.at[peer], (peer, h)).wait_recv()
        return carry + norm_s[peer]

    norm_total = lax.fori_loop(1, S, norm_seq_wait, norm_sum[...])
    width = norm_total.shape[1]
    norm_mine = pltpu.roll(norm_total, lax.rem(width - s * R, width), axis=1)[0:4, 0:R]
    norm_g[...] = norm_mine
    once = jnp.where(h == 0, 1.0, 0.0).astype(F32)
    norm_sums = sums_of(norm_w[...], norm_m[...], norm_u[...], norm_mine)
    norm_sums = (norm_sums[0] * once, norm_sums[1] * once)

    row = lax.broadcasted_iota(jnp.int32, (8, 128), 0)
    column = lax.broadcasted_iota(jnp.int32, (8, 128), 1)
    both = jnp.zeros((8, 128), F32)
    for number, pair in enumerate((qkv_sums, out_sums, up_sums, down_sums, norm_sums)):
        for which in range(2):
            both = jnp.where((row == number) & (column == which), pair[which], both)
    squares[...] = both

    def sq_seq(i):
        return remote(squares, sq_s.at[s], sq_s_send.at[i], sq_s_recv.at[s], (seq_peer(i), h))

    def sq_seq_start(i, carry):
        sq_seq(i).start()
        return carry

    def sq_seq_wait(i, carry):
        peer = seq_peer(i)
        remote(squares, sq_s.at[peer], sq_s_send.at[i], sq_s_recv.at[peer], (peer, h)).wait_recv()
        return carry + sq_s[peer]

    def sq_seq_sent(i, carry):
        sq_seq(i).wait_send()
        return carry

    lax.fori_loop(1, S, sq_seq_start, 0)
    both = lax.fori_loop(1, S, sq_seq_wait, both)
    lax.fori_loop(1, S, sq_seq_sent, 0)
    squares[...] = both
    sq_to_x = remote(squares, sq_x, small_sem.at[4], small_sem.at[5], other_x)
    sq_to_x.start()
    sq_to_x.wait()
    both = both + sq_x[...]
    squares[...] = both
    sq_to_core = remote(squares, sq_c, small_sem.at[6], small_sem.at[7], other_core)
    sq_to_core.start()
    sq_to_core.wait()
    squares[...] = both + sq_c[...]

    grad_copies[1].wait_recv()
    grad_copies[3].start()
    for copies in (out_copies, grad_copies):
        keep, to_x, to_core, passed = copies
        keep.wait()
        to_x.wait_send()
        to_core.wait_send()
        passed.wait_send()
        to_core.wait_recv()
        passed.wait_recv()

    for chunk in range(2):

        @pl.when(h - 2 + chunk < 0)
        def _():
            halo_copy(chunk).wait_send()

        back_copy(chunk).wait_send()
    for kind in (QKV, OUT, UP, DOWN):
        gather_x(kind, mine).wait_send()
        gather_core(kind, mine_pair).wait_send()
        scatter_core(kind).wait_send()
        scatter_x(kind).wait_send()

    def drain(i, carry):
        norm_part(i).wait_send()
        norm_seq(i).wait_send()
        for kind in (QKV, OUT, UP, DOWN):
            gather_seq(kind, i).wait_send()
            scatter_seq(kind, i).wait_send()
        return carry

    lax.fori_loop(1, S, drain, 0)


def run_layer(mesh_sizes, tok, cot, frames, weights, moments, seconds):
    S, H = mesh_sizes
    rows_dev, width = tok.shape
    T = rows_dev // H
    R = weights[0].shape[1]
    assert H == 4 and 2 * T == MOST_FRAMES * FRAME_TOKENS and R * S == width
    hidden = weights[2].shape[1]
    any_space = pl.BlockSpec(memory_space=pl.ANY)
    vmem = pl.BlockSpec(memory_space=pltpu.VMEM)
    smem = pl.BlockSpec(memory_space=pltpu.SMEM)
    dma = pltpu.SemaphoreType.DMA
    out_shape = (
        jax.ShapeDtypeStruct((rows_dev, width), BF16),
        jax.ShapeDtypeStruct((rows_dev, width), BF16),
        *[jax.ShapeDtypeStruct(w.shape, F32) for w in weights],
        jax.ShapeDtypeStruct((8, 128), F32),
    )
    cols = {DOWN: hidden, UP: hidden, OUT: 128, QKV: 384}
    order = (DOWN, UP, OUT, QKV)
    scratch = [
        *[pltpu.VMEM((H, S, R, cols[kind]), BF16) for kind in (QKV, OUT, UP, DOWN)],
        pltpu.VMEM((S, 8, width), F32),
        pltpu.VMEM((8, width), F32),
        pltpu.VMEM((3 * T, width), BF16),
        pltpu.VMEM((T, width), BF16),
        pltpu.VMEM((3 * T, width), BF16),
        pltpu.VMEM((width, 3 * T), BF16),
        pltpu.VMEM((H, T, 128), BF16),
        pltpu.VMEM((H, 3 * T, 128), BF16),
        pltpu.VMEM((H, 3 * T, 128), BF16),
        pltpu.VMEM((H, T // TILE, KEYS, 2 * TILE), BF16),
        pltpu.VMEM((H, T, 128), BF16),
        pltpu.VMEM((T, width), F32),
        pltpu.VMEM((T, width), BF16),
        pltpu.VMEM((width, T), BF16),
        pltpu.VMEM((width, T), BF16),
        pltpu.VMEM((T, width), F32),
        pltpu.VMEM((T, width), F32),
        pltpu.VMEM((T, hidden), F32),
        pltpu.VMEM((T, hidden), F32),
        pltpu.VMEM((T, hidden), BF16),
        pltpu.VMEM((T, hidden), BF16),
        pltpu.VMEM((T, width), BF16),
        pltpu.VMEM((T, width), BF16),
        pltpu.VMEM((H, T, 128), BF16),
        pltpu.VMEM((3 * T, 128), F32),
        pltpu.VMEM((3 * T, 128), F32),
        pltpu.VMEM((H, T, 128), BF16),
        pltpu.VMEM((H, 3 * T, 128), BF16),
        pltpu.VMEM((H, 3 * T, 128), BF16),
        pltpu.VMEM((3 * T, width), F32),
        pltpu.VMEM((2 * T, width), BF16),
        pltpu.VMEM((2, T, width), BF16),
        *[pltpu.VMEM((H, S, R, cols[kind]), BF16) for kind in order],
        *[pltpu.VMEM((2, S, R, cols[kind]), BF16) for kind in order],
        *[pltpu.VMEM((S, R, cols[kind]), BF16) for kind in order],
        *[pltpu.VMEM((S, R, cols[kind]), BF16) for kind in order],
        pltpu.VMEM((8, width), F32),
        pltpu.VMEM((8, width), F32),
        pltpu.VMEM((8, width), F32),
        pltpu.VMEM((S, 8, width), F32),
        pltpu.VMEM((8, 128), F32),
        pltpu.VMEM((8, 128), F32),
        pltpu.VMEM((S, 8, 128), F32),
        dma((4,)),
        dma((2, 2)),
        dma((2, S)),
        dma((4, S)),
        dma((4, S)),
        dma((2, 4)),
        dma((2, 4)),
        dma((2, 4)),
        dma((2, 4)),
        dma((4, S)),
        dma((4, S)),
        dma((8,)),
        dma((S,)),
        dma((S,)),
        dma((S,)),
        dma((S,)),
        dma((2, 7)),
        dma((2, 2)),
    ]
    operands = [tok, cot, frames, *weights]
    for moment, second in zip(moments, seconds):
        operands += [moment, second]
    return pl.pallas_call(
        functools.partial(layer_kernel, S, H),
        out_shape=out_shape,
        in_specs=[any_space, any_space, smem] + [vmem] * (len(operands) - 3),
        out_specs=(any_space, any_space) + (vmem,) * 6,
        scratch_shapes=scratch,
        compiler_params=pltpu.CompilerParams(
            collective_id=0, has_side_effects=True, vmem_limit_bytes=63 * 2**20
        ),
        name="layer",
    )(*operands)


def update_kernel(*refs):
    grads, masters, firsts, seconds = refs[0:5], refs[5:10], refs[10:15], refs[15:20]
    squares = refs[20]
    outs, norms = refs[21:46], refs[46]
    roots = jnp.sqrt(squares[...])
    for number in range(5):
        outs_here = outs[5 * number : 5 * number + 5]
        ratio = roots[number : number + 1, 0:1] / roots[number : number + 1, 1:2]
        pieces = range(grads[number].shape[0]) if grads[number].ndim == 3 else (slice(None),)
        for piece in pieces:
            gradient, master = grads[number][piece], masters[number][piece]
            first, second, direction = lamb_direction(
                master, firsts[number][piece], seconds[number][piece], gradient
            )
            new_master = master - RATE * ratio * direction
            outs_here[0][piece] = gradient
            outs_here[1][piece] = first
            outs_here[2][piece] = second
            outs_here[3][piece] = new_master
            outs_here[4][piece] = new_master.astype(BF16)
    norms[...] = roots[0:5, 0:2]


def run_update(grads, masters, firsts, seconds, squares):
    vmem = pl.BlockSpec(memory_space=pltpu.VMEM)
    operands = [*grads, *masters, *firsts, *seconds, squares]
    out_shape = []
    for grad in grads:
        out_shape += [jax.ShapeDtypeStruct(grad.shape, F32)] * 4 + [jax.ShapeDtypeStruct(grad.shape, BF16)]
    out_shape.append(jax.ShapeDtypeStruct((5, 2), F32))
    return pl.pallas_call(
        update_kernel,
        out_shape=tuple(out_shape),
        in_specs=[vmem] * len(operands),
        out_specs=(vmem,) * len(out_shape),
        name="update",
    )(*operands)


def local(mesh_sizes, *arrays):
    tokens, cotangent, frames = arrays[0:3]
    tensors = [list(arrays[3 + 3 * i : 6 + 3 * i]) for i in range(5)]
    for i in (1, 3):
        tensors[i] = [array.T for array in tensors[i]]
    masters, firsts, seconds = ([tensor[i] for tensor in tensors] for i in range(3))
    results = run_layer(mesh_sizes, tokens, cotangent, frames, masters, firsts, seconds)
    block_out, input_grad, grads, squares = results[0], results[1], results[2:7], results[7]
    updated = run_update(grads, masters, firsts, seconds, squares)
    outs = [block_out, input_grad.astype(F32)]
    for i in range(5):
        five = updated[5 * i : 5 * i + 5]
        outs += [array.T for array in five] if i in (1, 3) else list(five)
    outs.append(updated[25])
    return tuple(outs)


def solution(mesh):
    qkv, turned, straight, row = P(None, "seq", "head"), P("head", "seq"), P("seq", "head"), P(None, "seq")
    kinds = (qkv, turned, straight, turned, row)
    in_specs = [P("seq", None), P("seq", None), P()]
    out_specs = [P("seq", None), P("seq", None)]
    for kind in kinds:
        in_specs += [kind] * 3
        out_specs += [kind] * 5
    out_specs.append(P())
    return jax.shard_map(
        functools.partial(local, (mesh.shape["seq"], mesh.shape["head"])),
        mesh=mesh,
        in_specs=tuple(in_specs),
        out_specs=tuple(out_specs),
        check_vma=False,
    )
```

time: 1130 us -> 238 us (0.21)
  waiting for transfers between devices: 528 us -> 0 us
  Pallas kernels: 0 us -> 230 us
  matrix products: 207 us -> 0 us
  blocking collectives: 194 us -> 0 us
  other arithmetic: 149 us -> 4.35 us
  local copies, waits for them, and re-layouts: 28.5 us -> 2.65 us
  between operations: 19.1 us -> 0.69 us
    psum x3 -> x0, waiting for transfers between devices: 287 us -> none  [the longest x1 153 us: local(): lax.psum(jnp.dot(active_low, full_down, preferred_element_type=jnp.float3...]
    pallas_call x0 -> x2, Pallas kernels: none -> 230 us  [the longest x1 227 us: run_layer(): pl.pallas_call(functools.partial(layer_kernel, S, H), out_shape=out_shape...]
    dot_general x18 -> x0, matrix products: 207 us -> none  [the longest x1 50.7 us: local(): jnp.einsum('qhd,khd->hqk', grad_att_heads, value_heads, preferred_element...]
    all_gather x5 -> x0, blocking collectives: 154 us -> none  [the longest x1 37.6 us: local(): lax.all_gather(copies[1], 'seq', axis=1, tiled=True)]
    unnamed x10 -> x0, waiting for transfers between devices: 135 us -> none
    reduce_scatter x3 -> x0, waiting for transfers between devices: 77.4 us -> none  [the longest x1 63.7 us: local(): lax.psum_scatter(grad_down, 'seq', scatter_dimension=1, tiled=True)]
    convert_element_type x11 -> x1, other arithmetic: 65.6 us -> 4.35 us  [local(): outs = [block_out, input_grad.astype(F32)]]
    reduce_sum x15 -> x0, other arithmetic: 51.5 us -> none  [the longest x1 24.1 us: local(): jnp.sum(jnp.exp(scores - highest[..., None]), axis=-1)]
  transfers between devices with their start and end apart: 10 -> 0, of which waited for: 8 -> 0; matrix products, arithmetic and copies ran while one was open for 21% -> 0% of each run, Pallas kernels for 0% -> 0%
where the time goes in v1:
time: 238 us
  Pallas kernels  230 us (97%)
  other arithmetic  4.35 us (2%)
  local copies, waits for them, and re-layouts  2.65 us (1%)
    pallas_call x1, Pallas kernels, run_layer(): pl.pallas_call(functools.partial(layer_kernel, S, H), out_shape=out_shape...  227 us

profile of v1, /device:TPU:0, one launch (start us, length us, event | category | flops | bytes accessed | tf_op | source)
XLA Modules:
  0.0 237.9 jit_solution(317871962375018163)
XLA Ops:
  0.7 227.4 %layer.1 = (bf16[2048,512]{1,0:T(8,128)(2,1)}, bf16[2048,512]{1,0:T(8,128)(2,1)}, f32[3,64,128]{2,1,0:T(8,128)}, f32[64,128]{1,0:T(8,128)}, f32[64,512]{1,0:T(8,...) custom-call(bf16[2048,512]{1,0:T(8,128)(2,1)} %tok.1, bf16[2048,512]{1,0:T(8,128)(2,1)} %cot.1, ...), custom_call_target="tpu_custom_call" | custom-call | tf_op jit(solution)/shard_map/layer/pallas_call | solution.py:1003
  228.1 0.0 copy-start
  228.1 4.3 %convert_element_type.3 = f32[2048,512]{1,0:T(8,128)} convert(bf16[2048,512]{1,0:T(8,128)(2,1)} %get-tuple-element.63) | non-fusion elementwise | flops 1048576 | bytes 6291456 | tf_op jit(solution)/shard_map/convert_element_type | solution.py:1064
  232.4 2.8 %update.1 = (f32[3,64,128]{2,1,0:T(8,128)}, f32[3,64,128]{2,1,0:T(8,128)}, f32[3,64,128]{2,1,0:T(8,128)}, f32[3,64,128]{2,1,0:T(8,128)}, bf16[3,64,128]{2,1,0:T(...) custom-call(f32[3,64,128]{2,1,0:T(8,128)} %get-tuple-element.64.refs, ...), custom_call_target="tpu_custom_call" | custom-call | tf_op jit(solution)/shard_map/update/pallas_call | solution.py:1046
  235.3 1.3 copy.46
  236.6 0.0 copy-done
  236.6 1.3 copy.48
Async XLA Ops:
  228.1 8.5 %copy-start = (bf16[2048,512]{1,0:T(8,128)(2,1)S(1)}, bf16[2048,512]{1,0:T(8,128)(2,1)}, u32[]{:S(2)}) copy-start(bf16[2048,512]{1,0:T(8,128)(2,1)} %get-tuple-element.152) | copy-start | bytes 6291460
